TPU v7x, 512 devices: a whole 4x8x8 slice. The times are simulated.
512 devices in a mesh: dp: 16 (over z, core), tensor: 32 (over x, y).
Axes of the slice: x: 4, y: 8, z: 8, core: 2. Of those that a mesh axis runs over, the one named last changes fastest.
Arguments:
- activations: bfloat16 [12288, 4096], P('dp', 'tensor'), may hold values from -6 to 6
- out_grads_t: bfloat16 [5504, 12288], P('tensor', 'dp'), may hold values from -6 to 6
- in_basis: bfloat16 [4096, 4096], P(None, 'tensor'), may hold values from -0.09375 to 0.09375
- out_basis_t: bfloat16 [5504, 5504], P('tensor'), may hold values from -0.078125 to 0.078125
- query_proj: bfloat16 [4, 5504, 4096], P(None, 'tensor', 'dp'), may hold values from -6 to 6
- eigvals: float32 [5504, 4096], P('tensor', 'dp'), may hold values from 0.05 to 5
- damping: float32 [1], replicated, may hold values from 0.05 to 0.2
- lengths: int32 [96], P('dp'), may hold values from 1 to 128, 7680 in all
Outputs:
- scores: float32 [96, 4], P('dp')
Inputs may be any that keep to these rules, and one draw needn't show every extreme that they name: `lengths`: the largest token count is exactly 128.
All inputs are finite; a program needn't handle non-finite values. No bound on the sum of `lengths` on one device may be relied on, other than what follows from the above.
Results may differ from a plain program's by a relative error of at most 0.006.
Values may be sent and summed in bfloat16 or wider, within the bound.
No kernel may reach another device: no remote copies, remote signals or barrier semaphores. Data moves between devices by JAX's collectives and lax.ppermute only.
A program may use at most 128 MiB of HBM per device.

v0:
```python
import jax
import jax.numpy as jnp
from jax import lax
from jax.sharding import PartitionSpec as P


def local(activations, out_grads_t, in_basis, out_basis_t, query_proj, eigvals, damping, lengths):
    full_act = lax.all_gather(activations, "tensor", axis=1, tiled=True)
    act_local = jnp.dot(full_act, in_basis, preferred_element_type=jnp.float32).astype(jnp.bfloat16)
    act_proj = lax.all_gather(act_local, "tensor", axis=1, tiled=True)
    token_rows = full_act.shape[0]
    width = out_basis_t.shape[0]
    grad_full = jnp.dot(
        out_basis_t,
        lax.all_gather(out_grads_t, "tensor", axis=0, tiled=True),
        preferred_element_type=jnp.float32,
    )
    seq_count = lengths.shape[0]
    seq_len = token_rows // seq_count
    position = lax.broadcasted_iota(jnp.int32, (seq_count, seq_len), 1)
    keep = (position < lengths[:, None]).astype(jnp.float32).reshape(1, token_rows)
    grad_proj = (grad_full * keep).astype(jnp.bfloat16)
    scaled = (query_proj.astype(jnp.float32) / (eigvals + damping[0])).astype(jnp.bfloat16)
    projected = jnp.einsum(
        "jst,std->sjd",
        grad_proj.reshape(width, seq_count, seq_len),
        act_proj.reshape(seq_count, seq_len, act_proj.shape[1]),
        preferred_element_type=jnp.float32,
    )
    partial_value = jnp.einsum(
        "sij,qij->sq",
        projected,
        lax.all_gather(scaled, "dp", axis=2, tiled=True).astype(jnp.float32),
    )
    totals = lax.psum(partial_value, "tensor")
    norm_factor = (act_proj.shape[1] * out_basis_t.shape[1] * seq_len) ** (-0.5)
    return totals * norm_factor


def solution(mesh):
    placed = (
        P("dp", "tensor"),
        P("tensor", "dp"),
        P(None, "tensor"),
        P("tensor", None),
        P(None, "tensor", "dp"),
        P("tensor", "dp"),
        P(),
        P("dp"),
    )
    return jax.shard_map(
        local, mesh=mesh, in_specs=placed, out_specs=P("dp", None), check_vma=False
    )
```

profile of v0, /device:TPU:64, one launch (start us, length us, event | category | flops | bytes accessed | tf_op | source)
XLA Modules:
  0.0 474.7 jit_solution(10755105774203012612)
XLA Ops:
  6.5 0.0 copy-start
  6.5 0.0 copy-start.2
  6.5 0.0 copy-start.1
  6.5 0.0 copy-start.3
  6.5 0.0 all-gather.6.cloned.1.call-start
  6.6 0.7 all-gather.6.cloned.1.call-update
  7.3 0.0 all-gather.12.cloned.1.call-start
  7.3 0.7 all-gather.12.cloned.1.call-update
  8.0 0.0 all-gather.8.cloned.1.call-start
  8.1 104.2 %all-gather.6.cloned.1.call-done = bf16[768,4096]{1,0:T(8,128)(2,1)} async-done(((bf16[768,128]{1,0:T(8,128)(2,1)}), bf16[768,4096]{1,0:T(8,128)(2,1)}) %all-gather.6.cloned.1.call-update) | async-done | bytes 6291472 | tf_op jit(solution)/shard_map/all_gather | solution.py:8
  112.3 5.5 %convolution_convert_fusion = bf16[768,128]{1,0:T(8,128)(2,1)} fusion(bf16[768,4096]{1,0:T(8,128)(2,1)} %all-gather.6.cloned.1.call-done, bf16[4096,128]{1,0:T(8,128)(2,1)} %param.10), kind=kOutput, calls=%fused_computation.4 | convolution fusion | flops 805404672 | bytes 7536640 | tf_op jit(solution)/shard_map/dot_general | solution.py:9
  117.8 0.0 all-gather.8.cloned.1.call-update
  117.8 0.0 all-gather.10.cloned.1.call-start
  118.5 0.0 copy-done.2
  118.5 0.0 copy-done.1
  118.5 0.9 fusion.6
  119.5 0.0 all-gather.10.cloned.1.call-update
  119.5 0.0 copy-done.3
  119.5 0.1 convert_bitcast_fusion
  119.6 100.5 %all-gather.12.cloned.1.call-done = bf16[32,172,768]{2,1,0:T(8,128)(2,1)} async-done(((bf16[1,172,768]{2,1,0:T(8,128)(2,1)}), bf16[32,172,768]{2,1,0:T(8,128)(2,1)}) %all-gather.12.cloned.1.call-update) | async-done | bytes 8454160 | tf_op jit(solution)/shard_map/all_gather | solution.py:15
  220.1 12.5 %reshape.30 = bf16[5504,768]{1,0:T(8,128)(2,1)} reshape(bf16[32,172,768]{2,1,0:T(8,128)(2,1)} %all-gather.12.cloned.1.call-done) | data formatting | bytes 16908288
  232.6 0.0 copy-done
  232.6 5.2 %fusion.2 = bf16[172,768]{1,0:T(8,128)(2,1)S(1)} fusion(bf16[172,5504]{1,0:T(8,128)(2,1)S(1)} %copy-done, bf16[5504,768]{1,0:T(8,128)(2,1)} %reshape.30, f32[768]{0:T(1024)S(1)} %convert_bitcast_fusion), kind=kOutput, calls=%fused_computation.3 | convolution fusion | flops 1454376960 | bytes 10614784 | tf_op jit(solution)/shard_map/dot_general | solution.py:13
  237.7 0.3 reshape.26
  238.0 80.5 %all-gather.8.cloned.1.call-done = bf16[768,4096]{1,0:T(8,128)(2,1)} async-done(((bf16[768,128]{1,0:T(8,128)(2,1)}), bf16[768,4096]{1,0:T(8,128)(2,1)}) %all-gather.8.cloned.1.call-update) | async-done | bytes 6291472 | tf_op jit(solution)/shard_map/all_gather | solution.py:10
  318.6 8.5 %fusion.7 = bf16[6,172,4096]{2,1,0:T(8,128)(2,1)} fusion(bf16[6,128,4096]{2,1,0:T(8,128)(2,1)} %bitcast.14, bf16[172,6,128]{2,1,0:T(8,128)(2,1)S(1)} %reshape.26), kind=kOutput, calls=%fused_computation.8 | convolution fusion | flops 1082130432 | bytes 15009792 | tf_op jit(solution)/shard_map/jst,std->sjd/dot_general | solution.py:24
  327.1 51.2 %all-gather.10.cloned.1.call-done = bf16[4,172,4096]{2,0,1:T(4,128)(2,1)} async-done(((bf16[4,172,256]{2,0,1:T(4,128)(2,1)}), bf16[4,172,4096]{2,0,1:T(4,128)(2,1)}) %all-gather.10.cloned.1.call-update) | async-done | bytes 5636112 | tf_op jit(solution)/shard_map/all_gather | solution.py:33
  378.3 15.5 %fusion.3 = f32[6,4]{0,1:T(4,128)S(1)} fusion(bf16[4,172,4096]{2,0,1:T(4,128)(2,1)} %all-gather.10.cloned.1.call-done, bf16[6,172,4096]{2,1,0:T(8,128)(2,1)} %fusion.7), kind=kOutput, calls=%fused_computation.5 | convolution fusion | flops 33816576 | bytes 14090336 | tf_op jit(solution)/shard_map/sij,qij->sq/dot_general | solution.py:30
  393.8 73.8 %psum.7 = f32[6,4]{0,1:T(4,128)S(1)} all-reduce(f32[6,4]{0,1:T(4,128)S(1)} %fusion.3), channel_id=1, replica_groups=mesh['dp'=16,'tensor'=32] {'tensor'}, use_global_device_ids=true, to_apply=%region_0.0 | all-reduce | flops 24 | bytes 192 | tf_op jit(solution)/shard_map/psum | solution.py:35
  467.6 0.6 broadcast_multiply_fusion
  (1 shorter events, 0.0 us)
Async XLA Ops:
  6.5 226.0 %copy-start = (bf16[172,5504]{1,0:T(8,128)(2,1)S(1)}, bf16[172,5504]{1,0:T(8,128)(2,1)}, u32[]{:S(2)}) copy-start(bf16[172,5504]{1,0:T(8,128)(2,1)} %param.11) | copy-start | bytes 5680132
  6.5 111.9 %copy-start.2 = (f32[172,256]{1,0:T(8,128)S(1)}, f32[172,256]{1,0:T(8,128)}, u32[]{:S(2)}) copy-start(f32[172,256]{1,0:T(8,128)} %param.13) | copy-start | bytes 528388
  6.5 112.0 %copy-start.1 = (bf16[4,172,256]{2,0,1:T(4,128)(2,1)S(1)}, bf16[4,172,256]{2,0,1:T(4,128)(2,1)}, u32[]{:S(2)}) copy-start(bf16[4,172,256]{2,0,1:T(4,128)(2,1)} %param.12) | copy-start | bytes 1056772
  6.5 112.9 %copy-start.3 = (s32[6]{0:T(128)S(1)}, s32[6]{0:T(128)}, u32[]{:S(2)}) copy-start(s32[6]{0:T(128)} %param.15) | copy-start | bytes 76
  6.5 105.7 %all-gather.6.cloned.1.call-start = ((), (), s32[]{:S(2)}) async-start(), calls=%async_computation | async-start | bytes 6488064 | tf_op jit(solution)/shard_map/all_gather | solution.py:8
  7.3 212.8 %all-gather.12.cloned.1.call-start = ((), (), s32[]{:S(2)}) async-start(), calls=%async_computation.3 | async-start | bytes 8921088 | tf_op jit(solution)/shard_map/all_gather | solution.py:15
  8.0 310.6 %all-gather.8.cloned.1.call-start = ((), (), s32[]{:S(2)}) async-start(), calls=%async_computation.1 | async-start | bytes 6488064 | tf_op jit(solution)/shard_map/all_gather | solution.py:10
  117.8 260.5 %all-gather.10.cloned.1.call-start = ((), (), s32[]{:S(2)}) async-start(), calls=%async_computation.2 | async-start | bytes 5988352 | tf_op jit(solution)/shard_map/all_gather | solution.py:33
Sparse Core Ops, SparseCore 0:
  10.4 101.8 all-gather.5
  115.4 104.6 all-gather.11
  223.1 95.4 all-gather.7
  320.5 57.7 all-gather.9
where the time goes:
time: 475 us
  waiting for transfers between devices  338 us (71%)
  blocking collectives  73.8 us (16%)
  matrix products  34.7 us (7%)
  between operations  13.8 us (3%)
  local copies, waits for them, and re-layouts  12.8 us (3%)
    all_gather x1, waiting for transfers between devices, local(): full_act = lax.all_gather(activations, 'tensor', axis=1, tiled=True)  104 us
    all_gather x1, waiting for transfers between devices, local(): lax.all_gather(out_grads_t, 'tensor', axis=0, tiled=True)  101 us
    all_gather x1, waiting for transfers between devices, local(): act_proj = lax.all_gather(act_local, 'tensor', axis=1, tiled=True)  80.5 us
    psum x1, blocking collectives, local(): totals = lax.psum(partial_value, 'tensor')  73.8 us
    all_gather x1, waiting for transfers between devices, local(): lax.all_gather(scaled, 'dp', axis=2, tiled=True).astype(jnp.float32)  51.2 us
    dot_general x1, matrix products, local(): jnp.einsum('sij,qij->sq', projected, lax.all_gather(scaled, 'dp', axis=2,...  15.5 us
    unnamed x9, local copies, waits for them, and re-layouts  12.5 us
  transfers between devices with their start and end apart: 4, of which 4 were waited for; matrix products, arithmetic and copies ran while one was open for 7% of the time, Pallas kernels for 0%

commit v1 on v0

--- a/solution.py
+++ b/solution.py
@@ -12,7 +12,10 @@
     width = out_basis_t.shape[0]
     grad_full = jnp.dot(
         out_basis_t,
-        lax.all_gather(out_grads_t, "tensor", axis=0, tiled=True),
+        jnp.concatenate(
+            lax.all_to_all(jnp.stack([out_grads_t] * lax.axis_size("tensor")), "tensor", 0, 0),
+            axis=0,
+        ),
         preferred_element_type=jnp.float32,
     )
     seq_count = lengths.shape[0]

time: 475 us -> 500 us (1.053)
  waiting for transfers between devices: 338 us -> 350 us
  starting transfers between devices: 0.15 us -> 8.24 us
    all_to_all x0 -> x1, waiting for transfers between devices: none -> 223 us  [local(): lax.all_to_all(jnp.stack([out_grads_t] * lax.axis_size('tensor')), 'tenso...]
    all_gather x1 -> x0, waiting for transfers between devices: 101 us -> none  [local(): lax.all_gather(out_grads_t, 'tensor', axis=0, tiled=True)]
    all_gather x1, waiting for transfers between devices: 80.5 us -> 0.02 us  [local(): act_proj = lax.all_gather(act_local, 'tensor', axis=1, tiled=True)]
    all_gather x1, waiting for transfers between devices: 51.2 us -> 21.5 us  [local(): lax.all_gather(scaled, 'dp', axis=2, tiled=True).astype(jnp.float32)]
    reshape x0 -> x1, local copies, waits for them, and re-layouts: none -> 12.6 us  [local(): jnp.concatenate(lax.all_to_all(jnp.stack([out_grads_t] * lax.axis_size('t...]
    unnamed x9 -> x10, local copies, waits for them, and re-layouts: 12.5 us -> 0.02 us
    all_to_all x0 -> x1, starting transfers between devices: none -> 8.16 us  [local(): lax.all_to_all(jnp.stack([out_grads_t] * lax.axis_size('tensor')), 'tenso...]
  transfers between devices with their start and end apart: 4 -> 4, of which waited for: 4 -> 3; matrix products, arithmetic and copies ran while one was open for 7% -> 6% of each run, Pallas kernels for 0% -> 0%
where the time goes in v1:
time: 500 us; the launch traced here: 499 us
  waiting for transfers between devices  350 us (70%)
  blocking collectives  73.8 us (15%)
  matrix products  34.8 us (7%)
  local copies, waits for them, and re-layouts  16.8 us (3%)
  between operations  13.8 us (3%)
  starting transfers between devices  8.24 us (2%)
    all_to_all x1, waiting for transfers between devices, local(): lax.all_to_all(jnp.stack([out_grads_t] * lax.axis_size('tensor')), 'tenso...  223 us
    all_gather x1, waiting for transfers between devices, local(): full_act = lax.all_gather(activations, 'tensor', axis=1, tiled=True)  105 us
    psum x1, blocking collectives, local(): totals = lax.psum(partial_value, 'tensor')  73.8 us
    all_gather x1, waiting for transfers between devices, local(): lax.all_gather(scaled, 'dp', axis=2, tiled=True).astype(jnp.float32)  21.5 us
    dot_general x1, matrix products, local(): jnp.einsum('sij,qij->sq', projected, lax.all_gather(scaled, 'dp', axis=2,...  15.5 us
    reshape x1, local copies, waits for them, and re-layouts, local(): jnp.concatenate(lax.all_to_all(jnp.stack([out_grads_t] * lax.axis_size('t...  12.6 us
  transfers between devices with their start and end apart: 4, of which 3 were waited for; matrix products, arithmetic and copies ran while one was open for 6% of the time, Pallas kernels for 0%

profile of v1, /device:TPU:64, one launch (start us, length us, event | category | flops | bytes accessed | tf_op | source)
XLA Modules:
  0.0 499.5 jit_solution(1430175037953232528)
XLA Ops:
  6.5 0.0 copy-start
  6.5 0.0 copy-start.2
  6.5 0.0 all-gather.4.cloned.1.call-start
  6.5 0.7 all-gather.4.cloned.1.call-update
  7.3 0.0 all-gather.6.cloned.1.call-start
  7.3 104.9 %all-gather.4.cloned.1.call-done = bf16[768,4096]{1,0:T(8,128)(2,1)} async-done(((bf16[768,128]{1,0:T(8,128)(2,1)}), bf16[768,4096]{1,0:T(8,128)(2,1)}) %all-gather.4.cloned.1.call-update) | async-done | bytes 6291472 | tf_op jit(solution)/shard_map/all_gather | solution.py:8
  112.3 5.5 %convolution_convert_fusion = bf16[768,128]{1,0:T(8,128)(2,1)} fusion(bf16[768,4096]{1,0:T(8,128)(2,1)} %all-gather.4.cloned.1.call-done, bf16[4096,128]{1,0:T(8,128)(2,1)} %param.10), kind=kOutput, calls=%fused_computation.4 | convolution fusion | flops 805404672 | bytes 7536640 | tf_op jit(solution)/shard_map/dot_general | solution.py:9
  117.8 0.0 all-gather.6.cloned.1.call-update
  117.8 0.0 copy-done.2
  117.8 3.9 stack.2
  121.7 0.0 copy-start.3
  121.7 0.0 copy-start.1
  121.7 0.0 copy-start.4
  121.7 8.2 %all-to-all-start = ((bf16[32,172,768]{2,1,0:T(8,128)(2,1)}), bf16[32,172,768]{2,1,0:T(8,128)(2,1)}, u32[]{:S(2)}, u32[]{:S(2)}) async-start(bf16[32,172,768]{2,1,0:T(8,128)(2,1)} %stack.2), calls=%async_computation | async-start | bytes 17301504 | tf_op jit(solution)/shard_map/all_to_all | solution.py:16
  129.9 0.0 all-gather.8.cloned.1.call-start
  130.6 0.0 copy-done.3
  130.6 0.0 copy-done.1
  130.6 0.9 fusion.6
  131.5 0.0 all-gather.8.cloned.1.call-update
  131.6 0.0 copy-done.4
  131.6 0.1 convert_bitcast_fusion
  131.6 223.2 %all-to-all-done = bf16[32,172,768]{2,1,0:T(8,128)(2,1)} async-done(((bf16[32,172,768]{2,1,0:T(8,128)(2,1)}), bf16[32,172,768]{2,1,0:T(8,128)(2,1)}, u32[]{:S(2)}, u32[]{:S(2)}) %all-to-all-start) | async-done | bytes 8454176 | tf_op jit(solution)/shard_map/all_to_all | solution.py:16
  354.8 12.6 %reshape.31 = bf16[5504,768]{1,0:T(8,128)(2,1)} reshape(bf16[32,172,768]{2,1,0:T(8,128)(2,1)} %all-to-all-done) | data formatting | bytes 16908288 | tf_op jit(solution)/shard_map/reshape | solution.py:15
  367.4 0.0 copy-done
  367.4 5.1 %fusion.2 = bf16[172,768]{1,0:T(8,128)(2,1)S(1)} fusion(bf16[172,5504]{1,0:T(8,128)(2,1)S(1)} %copy-done, bf16[5504,768]{1,0:T(8,128)(2,1)} %reshape.31, f32[768]{0:T(1024)S(1)} %convert_bitcast_fusion), kind=kOutput, calls=%fused_computation.3 | convolution fusion | flops 1454376960 | bytes 10614784 | tf_op jit(solution)/shard_map/dot_general | solution.py:13
  372.5 0.3 reshape.32
  372.8 0.0 all-gather.6.cloned.1.call-done
  372.8 8.7 %fusion.7 = bf16[6,172,4096]{2,1,0:T(8,128)(2,1)} fusion(bf16[6,128,4096]{2,1,0:T(8,128)(2,1)} %bitcast.13, bf16[172,6,128]{2,1,0:T(8,128)(2,1)S(1)} %reshape.32), kind=kOutput, calls=%fused_computation.8 | convolution fusion | flops 1082130432 | bytes 15009792 | tf_op jit(solution)/shard_map/jst,std->sjd/dot_general | solution.py:27
  381.5 21.5 %all-gather.8.cloned.1.call-done = bf16[4,172,4096]{2,0,1:T(4,128)(2,1)} async-done(((bf16[4,172,256]{2,0,1:T(4,128)(2,1)}), bf16[4,172,4096]{2,0,1:T(4,128)(2,1)}) %all-gather.8.cloned.1.call-update) | async-done | bytes 5636112 | tf_op jit(solution)/shard_map/all_gather | solution.py:36
  403.0 15.5 %fusion.3 = f32[6,4]{0,1:T(4,128)S(1)} fusion(bf16[4,172,4096]{2,0,1:T(4,128)(2,1)} %all-gather.8.cloned.1.call-done, bf16[6,172,4096]{2,1,0:T(8,128)(2,1)} %fusion.7), kind=kOutput, calls=%fused_computation.5 | convolution fusion | flops 33816576 | bytes 14090336 | tf_op jit(solution)/shard_map/sij,qij->sq/dot_general | solution.py:33
  418.5 73.8 %psum.7 = f32[6,4]{0,1:T(4,128)S(1)} all-reduce(f32[6,4]{0,1:T(4,128)S(1)} %fusion.3), channel_id=1, replica_groups=mesh['dp'=16,'tensor'=32] {'tensor'}, use_global_device_ids=true, to_apply=%region_0.0 | all-reduce | flops 24 | bytes 192 | tf_op jit(solution)/shard_map/psum | solution.py:38
  492.3 0.6 broadcast_multiply_fusion
  (1 shorter events, 0.0 us)
Async XLA Ops:
  6.5 360.8 %copy-start = (bf16[172,5504]{1,0:T(8,128)(2,1)S(1)}, bf16[172,5504]{1,0:T(8,128)(2,1)}, u32[]{:S(2)}) copy-start(bf16[172,5504]{1,0:T(8,128)(2,1)} %param.11) | copy-start | bytes 5680132
  6.5 111.3 %copy-start.2 = (bf16[172,768]{1,0:T(8,128)(2,1)S(1)}, bf16[172,768]{1,0:T(8,128)(2,1)}, u32[]{:S(2)}) copy-start(bf16[172,768]{1,0:T(8,128)(2,1)} %param.9) | copy-start | bytes 792580
  6.5 105.7 %all-gather.4.cloned.1.call-start = ((), (), s32[]{:S(2)}) async-start(), calls=%async_computation.1 | async-start | bytes 6488064 | tf_op jit(solution)/shard_map/all_gather | solution.py:8
  7.3 365.6 %all-gather.6.cloned.1.call-start = ((), (), s32[]{:S(2)}) async-start(), calls=%async_computation.2 | async-start | bytes 6488064 | tf_op jit(solution)/shard_map/all_gather | solution.py:10
  121.7 8.9 %copy-start.3 = (f32[172,256]{1,0:T(8,128)S(1)}, f32[172,256]{1,0:T(8,128)}, u32[]{:S(2)}) copy-start(f32[172,256]{1,0:T(8,128)} %param.13) | copy-start | bytes 528388
  121.7 8.9 %copy-start.1 = (bf16[4,172,256]{2,0,1:T(4,128)(2,1)S(1)}, bf16[4,172,256]{2,0,1:T(4,128)(2,1)}, u32[]{:S(2)}) copy-start(bf16[4,172,256]{2,0,1:T(4,128)(2,1)} %param.12) | copy-start | bytes 1056772
  121.7 9.9 %copy-start.4 = (s32[6]{0:T(128)S(1)}, s32[6]{0:T(128)}, u32[]{:S(2)}) copy-start(s32[6]{0:T(128)} %param.15) | copy-start | bytes 76
  121.7 233.1 %all-to-all-start = ((bf16[32,172,768]{2,1,0:T(8,128)(2,1)}), bf16[32,172,768]{2,1,0:T(8,128)(2,1)}, u32[]{:S(2)}, u32[]{:S(2)}) async-start(bf16[32,172,768]{2,1,0:T(8,128)(2,1)} %stack.2), calls=%async_computation | async-start | bytes 17301504 | tf_op jit(solution)/shard_map/all_to_all | solution.py:16
  129.9 273.1 %all-gather.8.cloned.1.call-start = ((), (), s32[]{:S(2)}) async-start(), calls=%async_computation.3 | async-start | bytes 5988352 | tf_op jit(solution)/shard_map/all_gather | solution.py:36
Sparse Core Ops, SparseCore 0:
  10.4 101.8 all-gather.3
  117.9 223.1 all-gather.5
  343.1 59.8 all-gather.7
